TPU v7x, 32 devices: a whole 2x2x4 slice. The times are simulated.
32 devices in a mesh: row: 4 (over x, core), col: 8 (over z, y).
Axes of the slice: x: 2, y: 2, z: 4, core: 2. Of those that a mesh axis runs over, the one named last changes fastest.
Arguments:
- local_ops: bfloat16 [8, 8, 2048, 2048], P('row', 'col'), as said below
- start_vecs: float32 [8, 8, 1024, 128], P('row', 'col'), may hold values from -6 to 6
- multipliers: float32 [8, 8, 1024, 128], P('row', 'col'), may hold values from -6 to 6
- dual_rhs: float32 [8, 8, 1024, 128], P('row', 'col'), may hold values from -48 to 48
- mode_traces: bfloat16 [8, 8, 6, 2048], P('row', 'col'), may hold values from -0.1875 to 0.1875
- coarse_mult: float32 [8, 8, 6, 128], P('row', 'col'), may hold values from -6 to 6
- coarse_rhs: float32 [8, 8, 6, 128], P('row', 'col'), may hold values from -6 to 6
- face_size: int32 [8, 8, 2], P('row', 'col'), may hold values from 0 to 512, as said below
- contact: int32 [8, 8, 2], P('row', 'col'), may hold values 0 or 1
- mode_count: int32 [8, 8], P('row', 'col'), may hold values from 0 to 6
Outputs:
- new_multipliers: float32 [8, 8, 1024, 128], P('row', 'col')
- power_vectors: float32 [8, 8, 1024, 128], P('row', 'col')
- column_norms: float32 [128], replicated
- new_coarse: float32 [8, 8, 6, 128], P('row', 'col')
Inputs may be any that keep to these rules, and one draw needn't show every extreme that they name: face_size[r, c, 0] counts the live multipliers of the face between subdomains (r, c) and (r, c + 1), face_size[r, c, 1] of the face between (r, c) and (r + 1, c): a multiple of 128 from 128 to 512 for inner faces, 0 for faces on the grid's last column or last row. `local_ops`: each local operator is symmetric.
All inputs are finite; a program needn't handle non-finite values. No bound on the sum of `contact` on one device may be relied on, other than what follows from the above.
Results may differ from a plain program's by a relative error of at most 0.0007.
The roundings to bfloat16 on the way count: a program that leaves them out, or rounds other values in their place, can miss the bound.
Values may be sent and summed in bfloat16 or wider, within the bound.
A program may use at most 128 MiB of HBM per device.

v0:
```python
import jax
import jax.numpy as jnp
from jax import lax
from jax.sharding import PartitionSpec as P

ITERS = 4


EPSILON = 1e-06


def shifted(value, axis, steps):
    count = lax.axis_size(axis)
    first, last = (max(0, -steps), min(count, count - steps))
    return lax.ppermute(value, axis, [(source, source + steps) for source in range(first, last)])


def operate(matrices, owned, live_mask, coarse):
    slot_width = owned.shape[1] // 2
    east_faces = owned[:, :slot_width]
    south_faces = owned[:, slot_width:]
    west_in = shifted(east_faces, "col", 1)
    north_edge = shifted(south_faces[-1:], "row", 1)
    north_in = jnp.concatenate([north_edge, south_faces[:-1]], 0)
    signed = jnp.concatenate([-west_in, east_faces, -north_in, south_faces], 1)
    product = jnp.einsum("sij,sjc->sic", matrices, signed, preferred_element_type=jnp.float32)
    coarse_gap = None
    if coarse is not None:
        traces, coarse_mult, coarse_rhs, mode_live = coarse
        columns = signed.shape[2]
        dual_part = signed.astype(jnp.float32)
        coarse_gap = (
            jnp.einsum("skm,smn->skn", traces, dual_part, precision=lax.Precision.HIGHEST)
            - coarse_rhs
        ) * mode_live
        coarse_part = jnp.einsum(
            "skm,skn->smn",
            traces,
            jnp.concatenate([coarse_mult, coarse_gap], 2),
            precision=lax.Precision.HIGHEST,
        )
        product = jnp.concatenate([product, coarse_part], 2)
    west_part = product[:, :slot_width]
    east_part = product[:, slot_width : 2 * slot_width]
    north_part = product[:, 2 * slot_width : 3 * slot_width]
    south_part = product[:, 3 * slot_width :]
    from_east = shifted(west_part, "col", -1)
    south_edge = shifted(north_part[:1], "row", -1)
    from_south = jnp.concatenate([north_part[1:], south_edge], 0)
    assembled = jnp.concatenate([east_part - from_east, south_part - from_south], 1)
    return (assembled * live_mask, coarse_gap)


def local_squares(images):
    return jnp.sum(images * images, axis=(0, 1))


def body(
    local_ops,
    start_vecs,
    multipliers,
    dual_rhs,
    mode_traces,
    coarse_mult,
    coarse_rhs,
    face_size,
    contact,
    mode_count,
):
    blocks = local_ops.shape[0]
    order_size = local_ops.shape[2]
    matrices = local_ops.reshape(blocks, order_size, order_size)
    owned_len = start_vecs.shape[2]
    columns = start_vecs.shape[3]
    slot_width = owned_len // 2
    modes = mode_traces.shape[2]
    position = lax.broadcasted_iota(jnp.int32, (blocks, 2, slot_width), 2)
    sizes = face_size.reshape(blocks, 2)
    live_mask = (position < sizes[:, :, None]).astype(jnp.float32).reshape(blocks, owned_len, 1)
    contact_mask = jnp.broadcast_to(
        contact.reshape(blocks, 2, 1) > 0, (blocks, 2, slot_width)
    ).reshape(blocks, owned_len, 1)
    mode_live = (lax.broadcasted_iota(jnp.int32, (blocks, modes), 1) < mode_count).astype(
        jnp.float32
    )[:, :, None]
    traces = mode_traces.reshape(blocks, modes, order_size).astype(jnp.float32) * mode_live
    masked_mult = coarse_mult.reshape(blocks, modes, columns) * mode_live
    rhs_coarse = coarse_rhs.reshape(blocks, modes, columns)
    coarse = (traces, masked_mult, rhs_coarse, mode_live)
    base = multipliers.reshape(blocks, owned_len, columns) * live_mask
    base_half = base.astype(jnp.bfloat16)
    vectors = start_vecs.reshape(blocks, owned_len, columns) * live_mask
    previous_local = jnp.zeros((columns,), jnp.float32)
    last_local = jnp.zeros((columns,), jnp.float32)
    for sweep in range(ITERS):
        images, unused = operate(matrices, vectors.astype(jnp.bfloat16), live_mask, None)
        previous_local = last_local
        last_local = local_squares(images)
        vectors = images
    assembled, coarse_gap = operate(matrices, base_half, live_mask, coarse)
    totals = lax.psum(jnp.stack([previous_local, last_local], 0), ("row", "col"))
    column_norms = jnp.sqrt((totals[1] + EPSILON) / (totals[0] + EPSILON))
    vectors = vectors / jnp.sqrt(totals[1] + EPSILON)
    penalty = jnp.max(column_norms)
    step_length = 1.9 / penalty
    rhs_dual = dual_rhs.reshape(blocks, owned_len, columns) * live_mask
    grad = (
        assembled[:, :, :columns]
        + assembled[:, :, columns : 2 * columns]
        + penalty * assembled[:, :, 2 * columns :]
        - rhs_dual
    )
    trial = base - step_length * grad
    new_multipliers = jnp.where(contact_mask, jnp.maximum(trial, 0.0), trial) * live_mask
    new_coarse = masked_mult + penalty * coarse_gap
    return (
        new_multipliers.reshape(blocks, 1, owned_len, columns),
        vectors.reshape(blocks, 1, owned_len, columns),
        column_norms,
        new_coarse.reshape(blocks, 1, modes, columns),
    )


def solution(mesh):
    placed = (
        P("row", "col", None, None),
        P("row", "col", None, None),
        P("row", "col", None, None),
        P("row", "col", None, None),
        P("row", "col", None, None),
        P("row", "col", None, None),
        P("row", "col", None, None),
        P("row", "col", None),
        P("row", "col", None),
        P("row", "col"),
    )
    return jax.shard_map(
        body,
        mesh=mesh,
        in_specs=placed,
        out_specs=(
            P("row", "col", None, None),
            P("row", "col", None, None),
            P(),
            P("row", "col", None, None),
        ),
        check_vma=False,
    )
```

profile of v0, /device:TPU:0, one launch (start us, length us, event | category | flops | bytes accessed | tf_op | source)
XLA Modules:
  0.0 279.5 jit_solution(12727515542897265449)
XLA Ops:
  1.4 1.6 copy.25
  3.8 4.9 %collective-permute-start = (bf16[2,512,128]{1,2,0:T(8,128)(2,1)S(1)}, bf16[2,512,128]{1,2,0:T(8,128)(2,1)S(1)}, u32[]{:S(2)}, u32[]{:S(2)}) collective-permute-start(bf16[2,512,128]{1,2,0:T(8,128)(2,1)S(1)} %get-tuple-element.48), channel_id=1, source_target_pairs={{0,1},{1,2},{2,3},{3,4},{4,5},{5,6},{6,7},{8,9},{9,10},{10,11},{11... | collective-permute-start | bytes 786440 | tf_op jit(solution)/shard_map/ppermute | solution.py:15
  11.2 3.0 %collective-permute-done = bf16[2,512,128]{1,2,0:T(8,128)(2,1)S(1)} collective-permute-done((bf16[2,512,128]{1,2,0:T(8,128)(2,1)S(1)}, bf16[2,512,128]{1,2,0:T(8,128)(2,1)S(1)}, u32[]{:S(2)}, u32[]{:S(2)}) %collective-permute-start) | collective-permute-done | bytes 262176 | tf_op jit(solution)/shard_map/ppermute | solution.py:15
  14.3 11.6 %fusion.10 = f32[2,2048,128]{1,2,0:T(8,128)S(1)} fusion(bf16[2,1,2048,2048]{3,2,1,0:T(8,128)(2,1)} %param.10, bf16[2,512,128]{1,2,0:T(8,128)(2,1)} %get-tuple-element.49, bf16[2,512,128]{1,2,0:T(8,128)(2,1)S(1)} %maximum_negate_fusion, bf16[2,512,128]{1,2,0:T(8,128)(2,1)S(1)} %get-tuple-element.48, bf16[2,512,128]{1,2,0:T(8,128)(2,1)S(1)} %neg.30), kind=kOutput, calls=%fused_computation.19 | convolution fusion | flops 2151677952 | bytes 19922944 | tf_op jit(solution)/shard_map/sij,sjc->sic/dot_general | solution.py:26
  28.6 2.1 collective-permute-done.3
  30.7 10.9 %collective-permute-done.2 = f32[2,512,128]{1,2,0:T(8,128)S(1)} collective-permute-done((f32[2,512,128]{1,2,0:T(8,128)S(1)}, f32[2,512,128]{1,2,0:T(8,128)S(1)}, u32[]{:S(2)}, u32[]{:S(2)}) %collective-permute-start.2) | collective-permute-done | bytes 524320 | tf_op jit(solution)/shard_map/ppermute | solution.py:15
  42.7 4.3 %collective-permute-start.4 = (bf16[2,512,128]{1,2,0:T(8,128)(2,1)S(1)}, bf16[2,512,128]{1,2,0:T(8,128)(2,1)S(1)}, u32[]{:S(2)}, u32[]{:S(2)}) collective-permute-start(bf16[2,512,128]{1,2,0:T(8,128)(2,1)S(1)} %get-tuple-element.44), channel_id=1, source_target_pairs={{0,1},{1,2},{2,3},{3,4},{4,5},{5,6},{6,7},{8,9},{9,10},{10,11},{11... | collective-permute-start | bytes 786440 | tf_op jit(solution)/shard_map/ppermute | solution.py:15
  50.9 11.6 %fusion.13 = f32[2,2048,128]{1,2,0:T(8,128)S(1)} fusion(bf16[2,1,2048,2048]{3,2,1,0:T(8,128)(2,1)} %param.10, bf16[2,512,128]{1,2,0:T(8,128)(2,1)} %get-tuple-element.45, bf16[2,512,128]{1,2,0:T(8,128)(2,1)S(1)} %maximum_negate_fusion.1, bf16[2,512,128]{1,2,0:T(8,128)(2,1)} %copy-done.9, bf16[2,512,128]{1,2,0:T(8,128)(2,1)S(1)} %neg.32), kind=kOutput, calls=%fused_computation.20 | convolution fusion | flops 2151677952 | bytes 19922944 | tf_op jit(solution)/shard_map/sij,sjc->sic/dot_general | solution.py:26
  65.2 3.2 %collective-permute-done.7 = f32[1,512,128]{1,2,0:T(8,128)S(1)} collective-permute-done((f32[1,512,128]{1,2,0:T(8,128)S(1)}, f32[1,512,128]{1,2,0:T(8,128)S(1)}, u32[]{:S(2)}, u32[]{:S(2)}) %collective-permute-start.7) | collective-permute-done | bytes 262176 | tf_op jit(solution)/shard_map/ppermute | solution.py:15
  68.5 11.1 %collective-permute-done.6 = f32[2,512,128]{1,2,0:T(8,128)S(1)} collective-permute-done((f32[2,512,128]{1,2,0:T(8,128)S(1)}, f32[2,512,128]{1,2,0:T(8,128)S(1)}, u32[]{:S(2)}, u32[]{:S(2)}) %collective-permute-start.6) | collective-permute-done | bytes 524320 | tf_op jit(solution)/shard_map/ppermute | solution.py:15
  80.6 4.7 %collective-permute-start.8 = (bf16[2,512,128]{1,2,0:T(8,128)(2,1)S(1)}, bf16[2,512,128]{1,2,0:T(8,128)(2,1)S(1)}, u32[]{:S(2)}, u32[]{:S(2)}) collective-permute-start(bf16[2,512,128]{1,2,0:T(8,128)(2,1)S(1)} %get-tuple-element.40), channel_id=1, source_target_pairs={{0,1},{1,2},{2,3},{3,4},{4,5},{5,6},{6,7},{8,9},{9,10},{10,11},{11... | collective-permute-start | bytes 786440 | tf_op jit(solution)/shard_map/ppermute | solution.py:15
  85.3 1.6 collective-permute-start.9
  87.7 3.0 %collective-permute-done.8 = bf16[2,512,128]{1,2,0:T(8,128)(2,1)S(1)} collective-permute-done((bf16[2,512,128]{1,2,0:T(8,128)(2,1)S(1)}, bf16[2,512,128]{1,2,0:T(8,128)(2,1)S(1)}, u32[]{:S(2)}, u32[]{:S(2)}) %collective-permute-start.8) | collective-permute-done | bytes 262176 | tf_op jit(solution)/shard_map/ppermute | solution.py:15
  90.8 11.6 %fusion.16 = f32[2,2048,128]{1,2,0:T(8,128)S(1)} fusion(bf16[2,1,2048,2048]{3,2,1,0:T(8,128)(2,1)} %param.10, bf16[2,512,128]{1,2,0:T(8,128)(2,1)} %get-tuple-element.41, bf16[2,512,128]{1,2,0:T(8,128)(2,1)S(1)} %maximum_negate_fusion.2, bf16[2,512,128]{1,2,0:T(8,128)(2,1)} %copy-done.10, bf16[2,512,128]{1,2,0:T(8,128)(2,1)S(1)} %neg.34), kind=kOutput, calls=%fused_computation.21 | convolution fusion | flops 2151677952 | bytes 19922944 | tf_op jit(solution)/shard_map/sij,sjc->sic/dot_general | solution.py:26
  109.1 9.9 %collective-permute-done.10 = f32[2,512,128]{1,2,0:T(8,128)} collective-permute-done((f32[2,512,128]{1,2,0:T(8,128)}, f32[2,512,128]{1,2,0:T(8,128)}, u32[]{:S(2)}, u32[]{:S(2)}) %collective-permute-start.10) | collective-permute-done | bytes 524320 | tf_op jit(solution)/shard_map/ppermute | solution.py:15
  119.0 1.7 slice_subtract_fusion.3
  122.9 4.6 %collective-permute-start.12 = (bf16[2,512,128]{1,2,0:T(8,128)(2,1)S(1)}, bf16[2,512,128]{1,2,0:T(8,128)(2,1)S(1)}, u32[]{:S(2)}, u32[]{:S(2)}) collective-permute-start(bf16[2,512,128]{1,2,0:T(8,128)(2,1)S(1)} %get-tuple-element.36), channel_id=1, source_target_pairs={{0,1},{1,2},{2,3},{3,4},{4,5},{5,6},{6,7},{8,9},{9,10},{10,11},{11... | collective-permute-start | bytes 786440 | tf_op jit(solution)/shard_map/ppermute | solution.py:15
  127.7 4.1 %collective-permute-done.12 = bf16[2,512,128]{1,2,0:T(8,128)(2,1)S(1)} collective-permute-done((bf16[2,512,128]{1,2,0:T(8,128)(2,1)S(1)}, bf16[2,512,128]{1,2,0:T(8,128)(2,1)S(1)}, u32[]{:S(2)}, u32[]{:S(2)}) %collective-permute-start.12) | collective-permute-done | bytes 262176 | tf_op jit(solution)/shard_map/ppermute | solution.py:15
  131.8 12.9 %fusion.19 = f32[2,2048,128]{1,2,0:T(8,128)} fusion(bf16[2,1,2048,2048]{3,2,1,0:T(8,128)(2,1)} %param.10, bf16[2,512,128]{1,2,0:T(8,128)(2,1)} %get-tuple-element.37, bf16[2,512,128]{1,2,0:T(8,128)(2,1)S(1)} %maximum_negate_fusion.3, bf16[2,512,128]{1,2,0:T(8,128)(2,1)S(1)} %get-tuple-element.36, bf16[2,512,128]{1,2,0:T(8,128)(2,1)S(1)} %neg.36), kind=kOutput, calls=%fused_computation.22 | convolution fusion | flops 2151677952 | bytes 19922944 | tf_op jit(solution)/shard_map/sij,sjc->sic/dot_general | solution.py:26
  149.8 2.0 collective-permute-done.15
  151.8 8.4 %collective-permute-done.14 = f32[2,512,128]{1,2,0:T(8,128)S(1)} collective-permute-done((f32[2,512,128]{1,2,0:T(8,128)S(1)}, f32[2,512,128]{1,2,0:T(8,128)S(1)}, u32[]{:S(2)}, u32[]{:S(2)}) %collective-permute-start.14) | collective-permute-done | bytes 524320 | tf_op jit(solution)/shard_map/ppermute | solution.py:15
  162.1 40.1 %psum.7 = f32[2,128]{1,0:T(2,128)S(1)} all-reduce(f32[2,128]{1,0:T(2,128)S(1)} %pad_maximum_fusion.4), channel_id=1, replica_groups=mesh['row'=4,'col'=8] {'row','col'}, use_global_device_ids=true, to_apply=%region_2.0 | all-reduce | flops 256 | bytes 2048 | tf_op jit(solution)/shard_map/psum | solution.py:101
  203.5 4.5 %collective-permute-start.16 = (bf16[2,512,128]{1,2,0:T(8,128)(2,1)S(1)}, bf16[2,512,128]{1,2,0:T(8,128)(2,1)S(1)}, u32[]{:S(2)}, u32[]{:S(2)}) collective-permute-start(bf16[2,512,128]{1,2,0:T(8,128)(2,1)S(1)} %get-tuple-element.52), channel_id=1, source_target_pairs={{0,1},{1,2},{2,3},{3,4},{4,5},{5,6},{6,7},{8,9},{9,10},{10,11},{11... | collective-permute-start | bytes 786440 | tf_op jit(solution)/shard_map/ppermute | solution.py:15
  210.1 2.8 %collective-permute-done.16 = bf16[2,512,128]{1,2,0:T(8,128)(2,1)S(1)} collective-permute-done((bf16[2,512,128]{1,2,0:T(8,128)(2,1)S(1)}, bf16[2,512,128]{1,2,0:T(8,128)(2,1)S(1)}, u32[]{:S(2)}, u32[]{:S(2)}) %collective-permute-start.16) | collective-permute-done | bytes 262176 | tf_op jit(solution)/shard_map/ppermute | solution.py:15
  213.7 11.7 %fusion.22 = f32[2,2048,128]{1,2,0:T(8,128)S(1)} fusion(bf16[2,1,2048,2048]{3,2,1,0:T(8,128)(2,1)} %param.10, bf16[2,512,128]{1,2,0:T(8,128)(2,1)} %get-tuple-element.53, bf16[2,512,128]{1,2,0:T(8,128)(2,1)} %maximum_negate_fusion.4, bf16[2,512,128]{1,2,0:T(8,128)(2,1)} %copy-done.8, bf16[2,512,128]{1,2,0:T(8,128)(2,1)} %neg.38), kind=kOutput, calls=%fused_computation.23 | convolution fusion | flops 2151677952 | bytes 19922944 | tf_op jit(solution)/shard_map/sij,sjc->sic/dot_general | solution.py:26
  225.4 2.1 fusion.30
  228.3 3.5 %fusion.75 = f32[2,2048,256]{1,2,0:T(8,128)S(1)} fusion(f32[2,6,2048]{2,0,1:T(2,128)S(1)} %convert_multiply_fusion, f32[2,6,128]{2,1,0:T(8,128)S(1)} %fusion.30, f32[2,6,128]{2,1,0:T(8,128)S(1)} %get-tuple-element.58), kind=kOutput, calls=%fused_computation.102 | convolution fusion | flops 75500544 | bytes 4304896 | tf_op jit(solution)/shard_map/skm,skn->smn/dot_general | solution.py:36
  237.2 2.5 copy.34
  239.9 2.4 fusion.69
  242.3 2.5 copy.36
  246.2 26.2 %collective-permute-done.18 = f32[2,512,384]{1,2,0:T(8,128)} collective-permute-done((f32[2,512,384]{1,2,0:T(8,128)}, f32[2,512,384]{1,2,0:T(8,128)}, u32[]{:S(2)}, u32[]{:S(2)}) %collective-permute-start.18) | collective-permute-done | bytes 1572896 | tf_op jit(solution)/shard_map/ppermute | solution.py:15
  272.4 3.3 %fusion.26 = (f32[2,512,384]{1,2,0:T(8,128)S(1)}, f32[2,512,384]{1,2,0:T(8,128)S(1)}) fusion(f32[2,512,384]{1,2,0:T(8,128)} %collective-permute-done.18, f32[2,2048,256]{1,2,0:T(8,128)} %copy-done.2, f32[2,2048,128]{1,2,0:T(8,128)S(1)} %fusion.22, f32[1,512,384]{1,2,0:T(8,128)} %collective-permute-done.19, f32[1,512,384]{1,2,0:T(8,128)} %get-tuple-element.18), kind=kLoop, calls=%fused_computation.25 | loop fusion | flops 1966080 | bytes 12582912 | tf_op jit(solution)/shard_map/sub | solution.py:50
  (114 shorter events, 47.0 us)
Async XLA Ops:
  3.8 10.4 %collective-permute-start = (bf16[2,512,128]{1,2,0:T(8,128)(2,1)S(1)}, bf16[2,512,128]{1,2,0:T(8,128)(2,1)S(1)}, u32[]{:S(2)}, u32[]{:S(2)}) collective-permute-start(bf16[2,512,128]{1,2,0:T(8,128)(2,1)S(1)} %get-tuple-element.48), channel_id=1, source_target_pairs={{0,1},{1,2},{2,3},{3,4},{4,5},{5,6},{6,7},{8,9},{9,10},{10,11},{11... | collective-permute-start | bytes 786440 | tf_op jit(solution)/shard_map/ppermute | solution.py:15
  8.7 2.4 collective-permute-start.1
  25.9 15.7 %collective-permute-start.2 = (f32[2,512,128]{1,2,0:T(8,128)S(1)}, f32[2,512,128]{1,2,0:T(8,128)S(1)}, u32[]{:S(2)}, u32[]{:S(2)}) collective-permute-start(f32[2,512,128]{1,2,0:T(8,128)S(1)} %slice.231), channel_id=1, source_target_pairs={{1,0},{2,1},{3,2},{4,3},{5,4},{6,5},{7,6},{9,8},{10,9},{11,10},{12... | collective-permute-start | bytes 1572872 | tf_op jit(solution)/shard_map/ppermute | solution.py:15
  27.3 3.4 %collective-permute-start.3 = (f32[1,512,128]{1,2,0:T(8,128)S(1)}, f32[1,512,128]{1,2,0:T(8,128)S(1)}, u32[]{:S(2)}, u32[]{:S(2)}) collective-permute-start(f32[1,512,128]{1,2,0:T(8,128)S(1)} %get-tuple-element.35), channel_id=1, source_target_pairs={{8,0},{16,8},{24,16},{9,1},{17,9},{25,17},{10,2},{18,10},{26,18},{... | collective-permute-start | bytes 786440 | tf_op jit(solution)/shard_map/ppermute | solution.py:15
  42.7 8.2 %copy-start.9 = (bf16[2,512,128]{1,2,0:T(8,128)(2,1)}, bf16[2,512,128]{1,2,0:T(8,128)(2,1)S(1)}, u32[]{:S(2)}) copy-start(bf16[2,512,128]{1,2,0:T(8,128)(2,1)S(1)} %get-tuple-element.44) | copy-start | bytes 786436
  42.7 8.2 %collective-permute-start.4 = (bf16[2,512,128]{1,2,0:T(8,128)(2,1)S(1)}, bf16[2,512,128]{1,2,0:T(8,128)(2,1)S(1)}, u32[]{:S(2)}, u32[]{:S(2)}) collective-permute-start(bf16[2,512,128]{1,2,0:T(8,128)(2,1)S(1)} %get-tuple-element.44), channel_id=1, source_target_pairs={{0,1},{1,2},{2,3},{3,4},{4,5},{5,6},{6,7},{8,9},{9,10},{10,11},{11... | collective-permute-start | bytes 786440 | tf_op jit(solution)/shard_map/ppermute | solution.py:15
  47.0 2.3 collective-permute-start.5
  62.6 17.0 %collective-permute-start.6 = (f32[2,512,128]{1,2,0:T(8,128)S(1)}, f32[2,512,128]{1,2,0:T(8,128)S(1)}, u32[]{:S(2)}, u32[]{:S(2)}) collective-permute-start(f32[2,512,128]{1,2,0:T(8,128)S(1)} %slice.240), channel_id=1, source_target_pairs={{1,0},{2,1},{3,2},{4,3},{5,4},{6,5},{7,6},{9,8},{10,9},{11,10},{12... | collective-permute-start | bytes 1572872 | tf_op jit(solution)/shard_map/ppermute | solution.py:15
  63.9 4.5 %collective-permute-start.7 = (f32[1,512,128]{1,2,0:T(8,128)S(1)}, f32[1,512,128]{1,2,0:T(8,128)S(1)}, u32[]{:S(2)}, u32[]{:S(2)}) collective-permute-start(f32[1,512,128]{1,2,0:T(8,128)S(1)} %get-tuple-element.31), channel_id=1, source_target_pairs={{8,0},{16,8},{24,16},{9,1},{17,9},{25,17},{10,2},{18,10},{26,18},{... | collective-permute-start | bytes 786440 | tf_op jit(solution)/shard_map/ppermute | solution.py:15
  80.6 10.2 %copy-start.10 = (bf16[2,512,128]{1,2,0:T(8,128)(2,1)}, bf16[2,512,128]{1,2,0:T(8,128)(2,1)S(1)}, u32[]{:S(2)}) copy-start(bf16[2,512,128]{1,2,0:T(8,128)(2,1)S(1)} %get-tuple-element.40) | copy-start | bytes 786436
  80.6 10.2 %collective-permute-start.8 = (bf16[2,512,128]{1,2,0:T(8,128)(2,1)S(1)}, bf16[2,512,128]{1,2,0:T(8,128)(2,1)S(1)}, u32[]{:S(2)}, u32[]{:S(2)}) collective-permute-start(bf16[2,512,128]{1,2,0:T(8,128)(2,1)S(1)} %get-tuple-element.40), channel_id=1, source_target_pairs={{0,1},{1,2},{2,3},{3,4},{4,5},{5,6},{6,7},{8,9},{9,10},{10,11},{11... | collective-permute-start | bytes 786440 | tf_op jit(solution)/shard_map/ppermute | solution.py:15
  85.3 2.4 collective-permute-start.9
  102.4 5.8 %copy-start.7 = (f32[2,2048,128]{1,2,0:T(8,128)}, f32[2,2048,128]{1,2,0:T(8,128)S(1)}, u32[]{:S(2)}) copy-start(f32[2,2048,128]{1,2,0:T(8,128)S(1)} %fusion.16) | copy-start | bytes 6291460
  103.3 15.7 %collective-permute-start.10 = (f32[2,512,128]{1,2,0:T(8,128)}, f32[2,512,128]{1,2,0:T(8,128)}, u32[]{:S(2)}, u32[]{:S(2)}) collective-permute-start(f32[2,512,128]{1,2,0:T(8,128)} %slice.249), channel_id=1, source_target_pairs={{1,0},{2,1},{3,2},{4,3},{5,4},{6,5},{7,6},{9,8},{10,9},{11,10},{12... | collective-permute-start | bytes 1572872 | tf_op jit(solution)/shard_map/ppermute | solution.py:15
  105.4 3.8 %collective-permute-start.11 = (f32[1,512,128]{1,2,0:T(8,128)}, f32[1,512,128]{1,2,0:T(8,128)}, u32[]{:S(2)}, u32[]{:S(2)}) collective-permute-start(f32[1,512,128]{1,2,0:T(8,128)} %get-tuple-element.27), channel_id=1, source_target_pairs={{8,0},{16,8},{24,16},{9,1},{17,9},{25,17},{10,2},{18,10},{26,18},{... | collective-permute-start | bytes 786440 | tf_op jit(solution)/shard_map/ppermute | solution.py:15
  120.7 6.8 %copy-start.15 = (s32[2,1]{0,1:T(1,128)S(1)}, s32[2,1]{0,1:T(1,128)}, u32[]{:S(2)}) copy-start(s32[2,1]{0,1:T(1,128)} %param.19) | copy-start | bytes 28
  120.7 6.9 %copy-start.12 = (f32[2,1,6,128]{3,1,2,0:T(1,128)S(1)}, f32[2,1,6,128]{3,1,2,0:T(1,128)}, u32[]{:S(2)}) copy-start(f32[2,1,6,128]{3,1,2,0:T(1,128)} %param.16) | copy-start | bytes 18436
  120.7 6.9 %copy-start.13 = (f32[2,1,6,128]{3,1,2,0:T(1,128)S(1)}, f32[2,1,6,128]{3,1,2,0:T(1,128)}, u32[]{:S(2)}) copy-start(f32[2,1,6,128]{3,1,2,0:T(1,128)} %param.15) | copy-start | bytes 18436
  121.6 6.1 %collective-permute-start.13 = (bf16[1,512,128]{1,2,0:T(8,128)(2,1)S(1)}, bf16[1,512,128]{1,2,0:T(8,128)(2,1)S(1)}, u32[]{:S(2)}, u32[]{:S(2)}) collective-permute-start(bf16[1,512,128]{1,2,0:T(8,128)(2,1)S(1)} %get-tuple-element.38), channel_id=1, source_target_pairs={{0,8},{8,16},{16,24},{1,9},{9,17},{17,25},{2,10},{10,18},{18,26},{... | collective-permute-start | bytes 393224 | tf_op jit(solution)/shard_map/ppermute | solution.py:15
  122.9 8.9 %collective-permute-start.12 = (bf16[2,512,128]{1,2,0:T(8,128)(2,1)S(1)}, bf16[2,512,128]{1,2,0:T(8,128)(2,1)S(1)}, u32[]{:S(2)}, u32[]{:S(2)}) collective-permute-start(bf16[2,512,128]{1,2,0:T(8,128)(2,1)S(1)} %get-tuple-element.36), channel_id=1, source_target_pairs={{0,1},{1,2},{2,3},{3,4},{4,5},{5,6},{6,7},{8,9},{9,10},{10,11},{11... | collective-permute-start | bytes 786440 | tf_op jit(solution)/shard_map/ppermute | solution.py:15
  131.8 17.9 %copy-start.11 = (bf16[2,1,6,2048]{3,0,2,1:T(2,128)(2,1)S(1)}, bf16[2,1,6,2048]{3,0,2,1:T(2,128)(2,1)}, u32[]{:S(2)}) copy-start(bf16[2,1,6,2048]{3,0,2,1:T(2,128)(2,1)} %param.14) | copy-start | bytes 147460
  144.8 15.4 %copy-start.6 = (f32[2,2048,128]{1,2,0:T(8,128)S(1)}, f32[2,2048,128]{1,2,0:T(8,128)}, u32[]{:S(2)}) copy-start(f32[2,2048,128]{1,2,0:T(8,128)} %fusion.19) | copy-start | bytes 6291460
  146.0 14.2 %collective-permute-start.14 = (f32[2,512,128]{1,2,0:T(8,128)S(1)}, f32[2,512,128]{1,2,0:T(8,128)S(1)}, u32[]{:S(2)}, u32[]{:S(2)}) collective-permute-start(f32[2,512,128]{1,2,0:T(8,128)S(1)} %slice.258), channel_id=1, source_target_pairs={{1,0},{2,1},{3,2},{4,3},{5,4},{6,5},{7,6},{9,8},{10,9},{11,10},{12... | collective-permute-start | bytes 1572872 | tf_op jit(solution)/shard_map/ppermute | solution.py:15
  148.4 3.4 %collective-permute-start.15 = (f32[1,512,128]{1,2,0:T(8,128)S(1)}, f32[1,512,128]{1,2,0:T(8,128)S(1)}, u32[]{:S(2)}, u32[]{:S(2)}) collective-permute-start(f32[1,512,128]{1,2,0:T(8,128)S(1)} %get-tuple-element.23), channel_id=1, source_target_pairs={{8,0},{16,8},{24,16},{9,1},{17,9},{25,17},{10,2},{18,10},{26,18},{... | collective-permute-start | bytes 786440 | tf_op jit(solution)/shard_map/ppermute | solution.py:15
  162.1 51.6 %copy-start.8 = (bf16[2,512,128]{1,2,0:T(8,128)(2,1)}, bf16[2,512,128]{1,2,0:T(8,128)(2,1)S(1)}, u32[]{:S(2)}) copy-start(bf16[2,512,128]{1,2,0:T(8,128)(2,1)S(1)} %get-tuple-element.52) | copy-start | bytes 786436
  202.3 7.1 %collective-permute-start.17 = (bf16[1,512,128]{1,2,0:T(8,128)(2,1)S(1)}, bf16[1,512,128]{1,2,0:T(8,128)(2,1)S(1)}, u32[]{:S(2)}, u32[]{:S(2)}) collective-permute-start(bf16[1,512,128]{1,2,0:T(8,128)(2,1)S(1)} %get-tuple-element.54), channel_id=1, source_target_pairs={{0,8},{8,16},{16,24},{1,9},{9,17},{17,25},{2,10},{10,18},{18,26},{... | collective-permute-start | bytes 393224 | tf_op jit(solution)/shard_map/ppermute | solution.py:15
  203.5 9.3 %collective-permute-start.16 = (bf16[2,512,128]{1,2,0:T(8,128)(2,1)S(1)}, bf16[2,512,128]{1,2,0:T(8,128)(2,1)S(1)}, u32[]{:S(2)}, u32[]{:S(2)}) collective-permute-start(bf16[2,512,128]{1,2,0:T(8,128)(2,1)S(1)} %get-tuple-element.52), channel_id=1, source_target_pairs={{0,1},{1,2},{2,3},{3,4},{4,5},{5,6},{6,7},{8,9},{9,10},{10,11},{11... | collective-permute-start | bytes 786440 | tf_op jit(solution)/shard_map/ppermute | solution.py:15
  231.7 2.7 copy-start.2
  233.2 39.2 %collective-permute-start.18 = (f32[2,512,384]{1,2,0:T(8,128)}, f32[2,512,384]{1,2,0:T(8,128)}, u32[]{:S(2)}, u32[]{:S(2)}) collective-permute-start(f32[2,512,384]{1,2,0:T(8,128)} %fusion.27), channel_id=1, source_target_pairs={{1,0},{2,1},{3,2},{4,3},{5,4},{6,5},{7,6},{9,8},{10,9},{11,10},{12... | collective-permute-start | bytes 4718600 | tf_op jit(solution)/shard_map/ppermute | solution.py:15
  235.8 4.0 %copy-start.14 = (s32[2,1,2]{2,1,0:T(1,128)S(1)}, s32[2,1,2]{2,1,0:T(1,128)}, u32[]{:S(2)}) copy-start(s32[2,1,2]{2,1,0:T(1,128)} %param.18) | copy-start | bytes 52
  235.8 10.3 %collective-permute-start.19 = (f32[1,512,384]{1,2,0:T(8,128)}, f32[1,512,384]{1,2,0:T(8,128)}, u32[]{:S(2)}, u32[]{:S(2)}) collective-permute-start(f32[1,512,384]{1,2,0:T(8,128)} %get-tuple-element.19), channel_id=1, source_target_pairs={{8,0},{16,8},{24,16},{9,1},{17,9},{25,17},{10,2},{18,10},{26,18},{... | collective-permute-start | bytes 2359304 | tf_op jit(solution)/shard_map/ppermute | solution.py:15
  276.9 2.6 copy-start.1
  (4 other events, 3.7 us)
where the time goes:
time: 282 us; the launch traced here: 280 us
  waiting for transfers between devices  92 us (33%)
  matrix products  65 us (23%)
  starting transfers between devices  42.9 us (15%)
  blocking collectives  40.1 us (14%)
  local copies, waits for them, and re-layouts  20.5 us (7%)
  other arithmetic  17 us (6%)
    ppermute x20, waiting for transfers between devices, shifted(): lax.ppermute(value, axis, [(source, source + steps) for source in range(f...  92 us
    dot_general x5, matrix products, operate(): jnp.einsum('sij,sjc->sic', matrices, signed, preferred_element_type=jnp.f...  59.5 us
    ppermute x20, starting transfers between devices, shifted(): lax.ppermute(value, axis, [(source, source + steps) for source in range(f...  42.9 us
    psum x1, blocking collectives, body(): lax.psum(jnp.stack([previous_local, last_local], 0), ('row', 'col'))  40.1 us
    unnamed x47, local copies, waits for them, and re-layouts  12.5 us
  transfers between devices with their start and end apart: 20, of which 17 were waited for; matrix products, arithmetic and copies ran while one was open for 5% of the time, Pallas kernels for 0%

commit v1 on v0

v1 whole, which is shorter than its diff:
```python
import functools
import jax
import jax.numpy as jnp
from jax import lax
from jax.experimental import pallas as pl
from jax.experimental.pallas import tpu as pltpu
from jax.sharding import PartitionSpec as P

ITERS = 4
EPSILON = 1e-06
LANES = 128
GRAIN = 128
MODE_ROWS = 8
TOP = 32767.0
TINY = 1e-30
WEST, EAST, NORTH, SOUTH = 0, 1, 2, 3
SIGN = (-1.0, 1.0, -1.0, 1.0)
MESH = pl.DeviceIdType.MESH


def kernel(
    mesh_rows,
    mesh_cols,
    ops_hbm,
    start_ref,
    mult_ref,
    rhs_ref,
    traces_ref,
    coarse_mult_ref,
    coarse_rhs_ref,
    size_ref,
    contact_ref,
    count_ref,
    new_mult_ref,
    power_ref,
    norms_ref,
    new_coarse_ref,
    ops,
    signed,
    first_out,
    own_prod,
    base_prod,
    base_grad,
    own_diag,
    far_diag,
    info_out,
    info_in,
    code_out,
    code_in,
    scale_out,
    scale_in,
    modes_out,
    modes_in,
    traces_own,
    live,
    sums_out,
    sums_col,
    sums_row,
    load_sems,
    first_send,
    first_recv,
    info_send,
    info_recv,
    code_send,
    code_recv,
    scale_send,
    scale_recv,
    modes_send,
    modes_recv,
    col_send,
    col_recv,
    row_send,
    row_recv,
):
    blocks, order_size, _ = ops.shape
    face = order_size // 4
    grains = face // GRAIN
    modes = traces_ref.shape[1]
    base_index = ITERS
    row = lax.axis_index("row")
    col = lax.axis_index("col")

    loads = [
        pltpu.make_async_copy(ops_hbm.at[s], ops.at[s], load_sems.at[s]) for s in range(blocks)
    ]
    for load in loads:
        load.start()

    barrier = pltpu.get_barrier_semaphore()
    for step in range(1, mesh_cols):
        pl.semaphore_signal(
            barrier,
            inc=1,
            device_id=(row, lax.rem(col + step, mesh_cols)),
            device_id_type=MESH,
        )
    for step in range(1, mesh_rows):
        pl.semaphore_signal(
            barrier,
            inc=1,
            device_id=(lax.rem(row + step, mesh_rows), col),
            device_id_type=MESH,
        )

    links = []
    for s in range(blocks):
        links.append((s, blocks + s, s, WEST, col > 0, (row, col - 1)))
        links.append((blocks + s, s, s, EAST, col < mesh_cols - 1, (row, col + 1)))
    north_slot, south_slot = 2 * blocks, 2 * blocks + 1
    links.append((north_slot, south_slot, 0, NORTH, row > 0, (row - 1, col)))
    links.append(
        (south_slot, north_slot, blocks - 1, SOUTH, row < mesh_rows - 1, (row + 1, col))
    )
    owner_links = [link for link in links if link[3] in (EAST, SOUTH)]
    far_links = [link for link in links if link[3] in (WEST, NORTH)]

    def rows_of(side):
        return pl.ds(side * face, face)

    def remote(src, dst, send_sem, recv_sem, device):
        return pltpu.make_async_remote_copy(
            src_ref=src,
            dst_ref=dst,
            send_sem=send_sem,
            recv_sem=recv_sem,
            device_id=device,
            device_id_type=MESH,
        )

    def first_copy(link):
        here, there, s, side, _, device = link
        far_s = s if side == EAST else 0
        return remote(
            first_out.at[here],
            signed.at[far_s, rows_of(side - 1), :],
            first_send.at[here],
            first_recv.at[there],
            device,
        )

    def first_arrival(link):
        here, _, s, side, _, device = link
        return remote(
            first_out.at[here],
            signed.at[s, rows_of(side), :],
            first_send.at[here],
            first_recv.at[here],
            device,
        )

    def plain_copy(src, dst, send_sems, recv_sems, link, index=None):
        here, there, device = link[0], link[1], link[5]
        if index is None:
            return remote(
                src.at[here], dst.at[there], send_sems.at[here], recv_sems.at[there], device
            )
        return remote(
            src.at[index, here],
            dst.at[index, there],
            send_sems.at[index, here],
            recv_sems.at[index, there],
            device,
        )

    def arrival(src, dst, send_sems, recv_sems, link, index=None):
        here, device = link[0], link[5]
        if index is None:
            return remote(
                src.at[here], dst.at[here], send_sems.at[here], recv_sems.at[here], device
            )
        return remote(
            src.at[index, here],
            dst.at[index, here],
            send_sems.at[index, here],
            recv_sems.at[index, here],
            device,
        )

    info_bufs = (info_out, info_in, info_send, info_recv)
    code_bufs = (code_out, code_in, code_send, code_recv)
    scale_bufs = (scale_out, scale_in, scale_send, scale_recv)
    modes_bufs = (modes_out, modes_in, modes_send, modes_recv)

    grain_start = lax.broadcasted_iota(jnp.int32, (8, LANES), 0) * GRAIN
    for s in range(blocks):
        for half in range(2):
            live[s, half] = (grain_start < size_ref[s, half]).astype(jnp.float32)
    for s in range(blocks):
        for half, side in ((0, EAST), (1, SOUTH)):
            for grain in range(grains):
                mask = live[s, half, grain : grain + 1, :]
                src = pl.ds(half * face + grain * GRAIN, GRAIN)
                dst = pl.ds(side * face + grain * GRAIN, GRAIN)
                signed[s, dst, 0:LANES] = (start_ref[s, src, :] * mask).astype(jnp.bfloat16)
                signed[s, dst, LANES : 2 * LANES] = (mult_ref[s, src, :] * mask).astype(
                    jnp.bfloat16
                )
    for link in owner_links:
        here, _, s, side = link[:4]
        first_out[here] = -signed[s, rows_of(side), :]
    for s in range(1, blocks):
        signed[s, rows_of(NORTH), :] = -signed[s - 1, rows_of(SOUTH), :]

    pl.semaphore_wait(barrier, mesh_cols - 1 + mesh_rows - 1)
    for link in owner_links:

        @pl.when(link[4])
        def _(link=link):
            first_copy(link).start()

    for link in far_links:

        @pl.when(jnp.logical_not(link[4]))
        def _(link=link):
            signed[link[2], rows_of(link[3]), :] = jnp.zeros((face, 2 * LANES), jnp.bfloat16)

    for link in owner_links:

        @pl.when(jnp.logical_not(link[4]))
        def _(link=link):
            here, _, s, side = link[:4]
            modes_in[here] = jnp.zeros(modes_in.shape[1:], jnp.float32)
            out_rows = pl.ds((side // 2) * face, face)
            power_ref[s, out_rows, :] = jnp.zeros((face, LANES), jnp.float32)
            base_grad[s, out_rows, :] = jnp.zeros((face, LANES), jnp.float32)

    traces_own[...] = jnp.zeros_like(traces_own)
    coarse_live = []
    for s in range(blocks):
        mask = (
            lax.broadcasted_iota(jnp.int32, (modes, LANES), 0) < count_ref[s, 0]
        ).astype(jnp.float32)
        coarse_live.append(mask)
        mode_mask = (
            lax.broadcasted_iota(jnp.int32, (modes, order_size), 0) < count_ref[s, 0]
        ).astype(jnp.float32)
        traces_own[s, 0:modes, :] = traces_ref[s].astype(jnp.float32) * mode_mask

    eye = lax.broadcasted_iota(jnp.int32, (GRAIN, LANES), 0) == lax.broadcasted_iota(
        jnp.int32, (GRAIN, LANES), 1
    )
    info_out[...] = jnp.zeros_like(info_out)
    for s in range(blocks):
        loads[s].wait()
        for side in range(4):
            links_here = [link for link in links if link[2] == s and link[3] == side]
            for grain in range(grains):
                at = side * face + grain * GRAIN
                block = ops[s, at : at + GRAIN, at : at + GRAIN].astype(jnp.float32)
                block = jnp.where(eye, block, 0.0)
                own_diag[s, at : at + GRAIN, :] = jnp.broadcast_to(
                    jnp.sum(block, axis=1, keepdims=True), (GRAIN, LANES)
                )
                for link in links_here:
                    info_out[link[0], 8 + grain : 9 + grain, :] = jnp.sum(
                        block, axis=0, keepdims=True
                    )
            for link in links_here:
                if side in (EAST, SOUTH):
                    info_out[link[0], 0:8, :] = live[s, side // 2]

    for link in far_links:

        @pl.when(link[4])
        def _(link=link):
            first_arrival(link).wait_recv()

    for link in links:

        @pl.when(link[4])
        def _(link=link):
            plain_copy(*info_bufs, link).start()

    def multiply(s, side, wide):
        columns = 2 * LANES if wide else LANES
        part = jnp.dot(
            ops[s, rows_of(side), :],
            signed[s, :, 0:columns],
            preferred_element_type=jnp.float32,
        )
        if SIGN[side] < 0:
            part = -part
        own_prod[s, rows_of(side), :] = part[:, 0:LANES]
        if wide:
            base_prod[s, rows_of(side), :] = part[:, LANES:]

    def encode(s, side, slot, index):
        product, offset = (base_prod, LANES) if index == base_index else (own_prod, 0)
        for grain in range(grains):
            at = pl.ds(side * face + grain * GRAIN, GRAIN)
            vector = signed[s, at, offset : offset + LANES].astype(jnp.float32) * SIGN[side]
            rest = product[s, at, :] - own_diag[s, at, :] * vector
            largest = jnp.max(jnp.abs(rest), axis=0, keepdims=True)
            inverse = jnp.where(largest > TINY, TOP / jnp.maximum(largest, TINY), 0.0)
            scale_out[index, slot, grain : grain + 1, :] = largest * (1.0 / TOP)
            code_out[index, slot, grain * GRAIN : (grain + 1) * GRAIN, :] = (
                jnp.round(rest * inverse).astype(jnp.int32).astype(jnp.int16)
            )

    def decode(s, side, slot, index, grain):
        product, offset = (base_prod, LANES) if index == base_index else (own_prod, 0)
        at = pl.ds(side * face + grain * GRAIN, GRAIN)
        inner = slice(grain * GRAIN, (grain + 1) * GRAIN)
        vector = signed[s, at, offset : offset + LANES].astype(jnp.float32) * SIGN[side]
        rest = (
            code_in[index, slot, inner, :].astype(jnp.int32).astype(jnp.float32)
            * scale_in[index, slot, grain : grain + 1, :]
        )
        return product[s, at, :] + far_diag[slot, inner, :] * vector + rest

    def send_codes(link, index):
        plain_copy(*scale_bufs, link, index).start()
        plain_copy(*code_bufs, link, index).start()

    def await_codes(link, index):
        arrival(*scale_bufs, link, index).wait_recv()
        arrival(*code_bufs, link, index).wait_recv()

    scale_out[...] = jnp.zeros_like(scale_out)
    sums_out[...] = jnp.zeros_like(sums_out)
    inner_faces = [(s, SOUTH) for s in range(blocks - 1)] + [
        (s, NORTH) for s in range(1, blocks)
    ]

    for sweep in range(ITERS):
        last = sweep == ITERS - 1
        wide = sweep == 0
        for link in links:
            here, _, s, side, cond, _ = link
            multiply(s, side, wide)
            if last and side in (EAST, SOUTH):
                continue

            @pl.when(cond)
            def _(link=link, here=here, s=s, side=side, sweep=sweep):
                encode(s, side, here, sweep)
                send_codes(link, sweep)

        for s, side in inner_faces:
            multiply(s, side, wide)

        if wide:
            for link in far_links:

                @pl.when(link[4])
                def _(link=link):
                    encode(link[2], link[3], link[0], base_index)
                    send_codes(link, base_index)

            for s in range(blocks):
                gap = jnp.dot(
                    traces_own[s].astype(jnp.bfloat16),
                    signed[s, :, LANES : 2 * LANES],
                    preferred_element_type=jnp.float32,
                )
                masked_rhs = coarse_rhs_ref[s] * coarse_live[s]
                targets = [link for link in far_links if link[2] == s]
                modes_own = modes_out.at[2 * blocks + 2 + s]
                modes_own[...] = jnp.zeros_like(modes_own)
                modes_own[0:modes, :] = coarse_mult_ref[s] * coarse_live[s]
                modes_own[MODE_ROWS : MODE_ROWS + modes, :] = gap[0:modes, :] - masked_rhs
                for link in targets:
                    here, side = link[0], link[3]
                    modes_out[here, 0 : 2 * MODE_ROWS, :] = modes_own[0 : 2 * MODE_ROWS, :]
                    for grain in range(grains):
                        at = side * face + grain * GRAIN
                        base_row = (2 + grain) * MODE_ROWS
                        modes_out[here, base_row : base_row + MODE_ROWS, :] = traces_own[
                            s, :, at : at + GRAIN
                        ]
            for link in far_links:

                @pl.when(link[4])
                def _(link=link):
                    plain_copy(*modes_bufs, link).start()

            for link in links:

                @pl.when(link[4])
                def _(link=link):
                    here = link[0]
                    arrival(*info_bufs, link).wait_recv()
                    for grain in range(grains):
                        line = info_in[here, 8 + grain : 9 + grain, :]
                        line = jnp.where(eye, jnp.broadcast_to(line, (GRAIN, LANES)), 0.0)
                        far_diag[here, grain * GRAIN : (grain + 1) * GRAIN, :] = (
                            jnp.broadcast_to(
                                jnp.sum(line, axis=1, keepdims=True), (GRAIN, LANES)
                            )
                        )

        def finish(s, side, grain, value, sweep=sweep, last=last):
            at = pl.ds(side * face + grain * GRAIN, GRAIN)
            if not last:
                signed[s, at, 0:LANES] = (value * SIGN[side]).astype(jnp.bfloat16)
            if side in (EAST, SOUTH):
                if sweep >= ITERS - 2:
                    total_row = sweep - (ITERS - 2)
                    sums_out[0, total_row : total_row + 1, :] += jnp.sum(
                        value * value, axis=0, keepdims=True
                    )
                if last:
                    out_at = pl.ds((side // 2) * face + grain * GRAIN, GRAIN)
                    power_ref[s, out_at, :] = value

        for s in range(blocks - 1):
            for grain in range(grains):
                mask = live[s, 1, grain : grain + 1, :]
                upper = pl.ds(SOUTH * face + grain * GRAIN, GRAIN)
                lower = pl.ds(NORTH * face + grain * GRAIN, GRAIN)
                value = (own_prod[s, upper, :] + own_prod[s + 1, lower, :]) * mask
                finish(s, SOUTH, grain, value)
                if not last:
                    finish(s + 1, NORTH, grain, value)
                if wide:
                    base_grad[s, pl.ds(face + grain * GRAIN, GRAIN), :] = (
                        base_prod[s, upper, :] + base_prod[s + 1, lower, :]
                    )

        for link in links:
            here, _, s, side, cond, _ = link
            if last and side in (WEST, NORTH):
                continue

            @pl.when(cond)
            def _(link=link, here=here, s=s, side=side, sweep=sweep, finish=finish):
                await_codes(link, sweep)
                for grain in range(grains):
                    if side in (EAST, SOUTH):
                        mask = live[s, side // 2, grain : grain + 1, :]
                    else:
                        mask = info_in[here, grain : grain + 1, :]
                    finish(s, side, grain, decode(s, side, here, sweep, grain) * mask)

    sums_col[col] = sums_out[0]
    col_copies = []
    for step in range(1, mesh_cols):
        copy = remote(
            sums_out.at[0],
            sums_col.at[col],
            col_send.at[step],
            col_recv.at[step],
            (row, lax.rem(col + step, mesh_cols)),
        )
        copy.start()
        col_copies.append(copy)

    for link in owner_links:

        @pl.when(link[4])
        def _(link=link):
            here, _, s, side = link[:4]
            await_codes(link, base_index)
            arrival(*modes_bufs, link).wait_recv()
            for grain in range(grains):
                out_at = pl.ds((side // 2) * face + grain * GRAIN, GRAIN)
                base_grad[s, out_at, :] = decode(s, side, here, base_index, grain)

    for copy in col_copies:
        copy.wait()
    sums_out[1] = jnp.sum(sums_col[...], axis=0)
    sums_row[row] = sums_out[1]
    row_copies = []
    for step in range(1, mesh_rows):
        copy = remote(
            sums_out.at[1],
            sums_row.at[row],
            row_send.at[step],
            row_recv.at[step],
            (lax.rem(row + step, mesh_rows), col),
        )
        copy.start()
        row_copies.append(copy)
    for copy in row_copies:
        copy.wait()
    totals = jnp.sum(sums_row[...], axis=0)
    previous = totals[0:1, :]
    newest = totals[1:2, :]
    column_norms = jnp.sqrt((newest + EPSILON) / (previous + EPSILON))
    norms_ref[...] = column_norms
    penalty = jnp.max(column_norms, axis=1, keepdims=True)
    step_length = 1.9 / penalty
    inverse_norm = 1.0 / jnp.sqrt(newest + EPSILON)

    def coefficients(buf):
        return buf[0:MODE_ROWS, :] + penalty * buf[MODE_ROWS : 2 * MODE_ROWS, :]

    own_coarse = [coefficients(modes_out.at[2 * blocks + 2 + s]) for s in range(blocks)]
    for s in range(blocks):
        new_coarse_ref[s] = own_coarse[s][0:modes, :]
    for s in range(blocks):
        for half, side in ((0, EAST), (1, SOUTH)):
            slot = blocks + s if side == EAST else south_slot
            local = side == SOUTH and s < blocks - 1
            far_coarse = own_coarse[s + 1] if local else coefficients(modes_in.at[slot])
            pair = jnp.concatenate([own_coarse[s], far_coarse], axis=0)
            hit = (contact_ref[s, half] > 0).astype(jnp.float32)
            for grain in range(grains):
                at = side * face + grain * GRAIN
                if local:
                    far_at = at - face
                    far_traces = traces_own[s + 1, :, far_at : far_at + GRAIN]
                else:
                    base_row = (2 + grain) * MODE_ROWS
                    far_traces = modes_in[slot, base_row : base_row + MODE_ROWS, :]
                both = jnp.concatenate(
                    [traces_own[s, :, at : at + GRAIN], -far_traces], axis=0
                )
                coarse_part = lax.dot_general(
                    both,
                    pair,
                    (((0,), (0,)), ((), ())),
                    precision=lax.Precision.HIGHEST,
                    preferred_element_type=jnp.float32,
                )
                out_at = pl.ds(half * face + grain * GRAIN, GRAIN)
                mask = live[s, half, grain : grain + 1, :]
                grad = (base_grad[s, out_at, :] + coarse_part - rhs_ref[s, out_at, :]) * mask
                trial = mult_ref[s, out_at, :] * mask - step_length * grad
                clipped = jnp.maximum(trial, 0.0)
                new_mult_ref[s, out_at, :] = jnp.where(hit > 0.0, clipped, trial) * mask
                power_ref[s, out_at, :] = power_ref[s, out_at, :] * inverse_norm

    for link in links:
        owner = link[3] in (EAST, SOUTH)

        @pl.when(link[4])
        def _(link=link, owner=owner):
            plain_copy(*info_bufs, link).wait_send()
            indices = list(range(ITERS - 1)) if owner else list(range(ITERS + 1))
            for index in indices:
                plain_copy(*scale_bufs, link, index).wait_send()
                plain_copy(*code_bufs, link, index).wait_send()
            if owner:
                first_copy(link).wait_send()
            else:
                plain_copy(*modes_bufs, link).wait_send()


def body(
    mesh_rows,
    mesh_cols,
    local_ops,
    start_vecs,
    multipliers,
    dual_rhs,
    mode_traces,
    coarse_mult,
    coarse_rhs,
    face_size,
    contact,
    mode_count,
):
    blocks = local_ops.shape[0]
    order_size = local_ops.shape[2]
    owned_len = start_vecs.shape[2]
    columns = start_vecs.shape[3]
    face = owned_len // 2
    modes = mode_traces.shape[2]
    slots = 2 * blocks + 2
    mode_height = (2 + face // GRAIN) * MODE_ROWS
    vmem = pl.BlockSpec(memory_space=pltpu.VMEM)
    smem = pl.BlockSpec(memory_space=pltpu.SMEM)
    dma = pltpu.SemaphoreType.DMA
    f32, bf16, i16 = jnp.float32, jnp.bfloat16, jnp.int16
    flops = 2 * blocks * order_size * order_size * columns * (ITERS + 1)
    new_mult, power, norms, new_coarse = pl.pallas_call(
        functools.partial(kernel, mesh_rows, mesh_cols),
        out_shape=(
            jax.ShapeDtypeStruct((blocks, owned_len, columns), f32),
            jax.ShapeDtypeStruct((blocks, owned_len, columns), f32),
            jax.ShapeDtypeStruct((1, columns), f32),
            jax.ShapeDtypeStruct((blocks, modes, columns), f32),
        ),
        in_specs=[pl.BlockSpec(memory_space=pl.ANY)] + [vmem] * 6 + [smem] * 3,
        out_specs=(vmem, vmem, vmem, vmem),
        scratch_shapes=[
            pltpu.VMEM((blocks, order_size, order_size), bf16),
            pltpu.VMEM((blocks, order_size, 2 * columns), bf16),
            pltpu.VMEM((slots, face, 2 * columns), bf16),
            pltpu.VMEM((blocks, order_size, columns), f32),
            pltpu.VMEM((blocks, order_size, columns), f32),
            pltpu.VMEM((blocks, owned_len, columns), f32),
            pltpu.VMEM((blocks, order_size, columns), f32),
            pltpu.VMEM((slots, face, columns), f32),
            pltpu.VMEM((slots, 16, columns), f32),
            pltpu.VMEM((slots, 16, columns), f32),
            pltpu.VMEM((ITERS + 1, slots, face, columns), i16),
            pltpu.VMEM((ITERS + 1, slots, face, columns), i16),
            pltpu.VMEM((ITERS + 1, slots, 8, columns), f32),
            pltpu.VMEM((ITERS + 1, slots, 8, columns), f32),
            pltpu.VMEM((slots + blocks, mode_height, columns), f32),
            pltpu.VMEM((slots, mode_height, columns), f32),
            pltpu.VMEM((blocks, MODE_ROWS, order_size), f32),
            pltpu.VMEM((blocks, 2, 8, columns), f32),
            pltpu.VMEM((2, 8, columns), f32),
            pltpu.VMEM((mesh_cols, 8, columns), f32),
            pltpu.VMEM((mesh_rows, 8, columns), f32),
            dma((blocks,)),
            dma((slots,)),
            dma((slots,)),
            dma((slots,)),
            dma((slots,)),
            dma((ITERS + 1, slots)),
            dma((ITERS + 1, slots)),
            dma((ITERS + 1, slots)),
            dma((ITERS + 1, slots)),
            dma((slots,)),
            dma((slots,)),
            dma((mesh_cols,)),
            dma((mesh_cols,)),
            dma((mesh_rows,)),
            dma((mesh_rows,)),
        ],
        compiler_params=pltpu.CompilerParams(
            collective_id=0, has_side_effects=True, vmem_limit_bytes=56 * 1024 * 1024
        ),
        cost_estimate=pl.CostEstimate(
            flops=flops, bytes_accessed=2 * blocks * order_size * order_size, transcendentals=0
        ),
    )(
        local_ops.reshape(blocks, order_size, order_size),
        start_vecs.reshape(blocks, owned_len, columns),
        multipliers.reshape(blocks, owned_len, columns),
        dual_rhs.reshape(blocks, owned_len, columns),
        mode_traces.reshape(blocks, modes, order_size),
        coarse_mult.reshape(blocks, modes, columns),
        coarse_rhs.reshape(blocks, modes, columns),
        face_size.reshape(blocks, 2),
        contact.reshape(blocks, 2),
        mode_count.reshape(blocks, 1),
    )
    return (
        new_mult.reshape(blocks, 1, owned_len, columns),
        power.reshape(blocks, 1, owned_len, columns),
        norms.reshape(columns),
        new_coarse.reshape(blocks, 1, modes, columns),
    )


def solution(mesh):
    wide = P("row", "col", None, None)
    sizes = dict(mesh.shape)
    return jax.shard_map(
        functools.partial(body, sizes["row"], sizes["col"]),
        mesh=mesh,
        in_specs=(wide,) * 7 + (P("row", "col", None), P("row", "col", None), P("row", "col")),
        out_specs=(wide, wide, P(), wide),
        check_vma=False,
    )
```

time: 282 us -> 114 us (0.40)
  Pallas kernels: 0 us -> 101 us
  waiting for transfers between devices: 92 us -> 0 us
  matrix products: 65 us -> 0 us
  starting transfers between devices: 42.9 us -> 0 us
  blocking collectives: 40.1 us -> 0 us
  other arithmetic: 17 us -> 0 us
  local copies, waits for them, and re-layouts: 20.5 us -> 12.2 us
    pallas_call x0 -> x1, Pallas kernels: none -> 101 us  [body(): pl.pallas_call(functools.partial(kernel, mesh_rows, mesh_cols), out_shape...]
    ppermute x20 -> x0, waiting for transfers between devices: 92 us -> none  [shifted(): lax.ppermute(value, axis, [(source, source + steps) for source in range(f...]
    dot_general x7 -> x0, matrix products: 65 us -> none  [the longest x5 59.5 us: operate(): jnp.einsum('sij,sjc->sic', matrices, signed, preferred_element_type=jnp.f...]
    ppermute x20 -> x0, starting transfers between devices: 42.9 us -> none  [shifted(): lax.ppermute(value, axis, [(source, source + steps) for source in range(f...]
    psum x1 -> x0, blocking collectives: 40.1 us -> none  [body(): lax.psum(jnp.stack([previous_local, last_local], 0), ('row', 'col'))]
    slice x18 -> x0, local copies, waits for them, and re-layouts: 7.9 us -> none  [the longest x5 3.72 us: operate(): east_faces = owned[:, :slot_width]]
    sub x5 -> x0, other arithmetic: 5.55 us -> none  [operate(): east_part - from_east]
    unnamed x47 -> x8, local copies, waits for them, and re-layouts: 12.5 us -> 11 us
  transfers between devices with their start and end apart: 20 -> 0, of which waited for: 17 -> 0; matrix products, arithmetic and copies ran while one was open for 5% -> 0% of each run, Pallas kernels for 0% -> 0%
where the time goes in v1:
time: 114 us
  Pallas kernels  101 us (89%)
  local copies, waits for them, and re-layouts  12.2 us (11%)
    pallas_call x1, Pallas kernels, body(): pl.pallas_call(functools.partial(kernel, mesh_rows, mesh_cols), out_shape...  101 us
    unnamed x8, local copies, waits for them, and re-layouts  11 us

profile of v1, /device:TPU:0, one launch (start us, length us, event | category | flops | bytes accessed | tf_op | source)
XLA Modules:
  0.0 113.7 jit_solution(10789477295408960501)
XLA Ops:
  0.6 1.3 %copy.24.count_ref = s32[2,1]{1,0:T(2,128)} copy(s32[2,1]{0,1:T(1,128)} %param.19) | data formatting | bytes 16 | tf_op args[9]
  1.9 0.7 copy.33
  2.6 0.6 copy.22.coarse_mult_ref
  3.2 0.7 copy.32
  3.9 0.6 copy.23.coarse_rhs_ref
  4.5 1.4 %copy.31 = bf16[2,1,6,2048]{3,2,0,1:T(8,128)(2,1)} copy(bf16[2,1,6,2048]{3,0,2,1:T(2,128)(2,1)} %param.14) | data formatting | bytes 98304 | tf_op args[4]
  6.0 100.8 %shard_map.129 = (f32[2,1024,128]{2,1,0:T(8,128)}, f32[2,1024,128]{2,1,0:T(8,128)}, f32[1,128]{1,0:T(1,128)}, f32[2,6,128]{2,1,0:T(8,128)}) custom-call(bf16[2,2048,2048]{2,1,0:T(8,128)(2,1)} %bitcast.29, f32[2,1024,128]{2,1,0:T(8,128)} %bitcast.30, f32[2,1024,128]{2,1,0:T(8,128)} %bitcast.31, f32[2,1024,128]{2,1,0:T(8,128)} %bitcast.32, ...), custom_call_target="tpu_custom_call" | custom-call | flops 10737418240 | bytes 16777216 | tf_op jit(solution)/shard_map/pallas_call | solution.py:567
  106.8 1.3 %copy.27 = f32[2,1,6,128]{3,1,2,0:T(1,128)} copy(f32[2,1,6,128]{3,2,0,1:T(8,128)} %bitcast.28) | data formatting | bytes 12288
  108.1 2.3 %copy.37 = f32[2,1,1024,128]{3,2,1,0:T(8,128)} copy(f32[2,1,1024,128]{3,2,1,0:T(8,128)} %bitcast.24) | data formatting | bytes 2097152
  110.3 2.3 %copy.38 = f32[2,1,1024,128]{3,2,1,0:T(8,128)} copy(f32[2,1,1024,128]{3,2,1,0:T(8,128)} %bitcast.23) | data formatting | bytes 2097152
  112.6 1.1 copy.39

commit v2 on v1

--- a/solution.py
+++ b/solution.py
@@ -41,6 +41,7 @@
     own_prod,
     base_prod,
     base_grad,
+    gap_grad,
     own_diag,
     far_diag,
     info_out,
@@ -127,24 +128,24 @@
             device_id_type=MESH,
         )
 
-    def first_copy(link):
+    def first_copy(link, group):
         here, there, s, side, _, device = link
         far_s = s if side == EAST else 0
         return remote(
-            first_out.at[here],
-            signed.at[far_s, rows_of(side - 1), :],
-            first_send.at[here],
-            first_recv.at[there],
+            first_out.at[group, here],
+            signed.at[far_s, rows_of(side - 1), pl.ds(group * LANES, LANES)],
+            first_send.at[group, here],
+            first_recv.at[group, there],
             device,
         )
 
-    def first_arrival(link):
+    def first_arrival(link, group):
         here, _, s, side, _, device = link
         return remote(
-            first_out.at[here],
-            signed.at[s, rows_of(side), :],
-            first_send.at[here],
-            first_recv.at[here],
+            first_out.at[group, here],
+            signed.at[s, rows_of(side), pl.ds(group * LANES, LANES)],
+            first_send.at[group, here],
+            first_recv.at[group, here],
             device,
         )
 
@@ -197,7 +198,10 @@
                 )
     for link in owner_links:
         here, _, s, side = link[:4]
-        first_out[here] = -signed[s, rows_of(side), :]
+        for group in range(2):
+            first_out[group, here] = -signed[
+                s, rows_of(side), group * LANES : (group + 1) * LANES
+            ]
     for s in range(1, blocks):
         signed[s, rows_of(NORTH), :] = -signed[s - 1, rows_of(SOUTH), :]
 
@@ -206,7 +210,7 @@
 
         @pl.when(link[4])
         def _(link=link):
-            first_copy(link).start()
+            first_copy(link, 0).start()
 
     for link in far_links:
 
@@ -246,8 +250,11 @@
             links_here = [link for link in links if link[2] == s and link[3] == side]
             for grain in range(grains):
                 at = side * face + grain * GRAIN
-                block = ops[s, at : at + GRAIN, at : at + GRAIN].astype(jnp.float32)
-                block = jnp.where(eye, block, 0.0)
+                whole = ops[s, at : at + GRAIN, at : at + GRAIN].astype(jnp.float32)
+                block = jnp.where(eye, whole, 0.0)
+                ops[s, at : at + GRAIN, at : at + GRAIN] = jnp.where(eye, 0.0, whole).astype(
+                    jnp.bfloat16
+                )
                 own_diag[s, at : at + GRAIN, :] = jnp.broadcast_to(
                     jnp.sum(block, axis=1, keepdims=True), (GRAIN, LANES)
                 )
@@ -263,7 +270,7 @@
 
         @pl.when(link[4])
         def _(link=link):
-            first_arrival(link).wait_recv()
+            first_arrival(link, 0).wait_recv()
 
     for link in links:
 
@@ -285,11 +292,10 @@
             base_prod[s, rows_of(side), :] = part[:, LANES:]
 
     def encode(s, side, slot, index):
-        product, offset = (base_prod, LANES) if index == base_index else (own_prod, 0)
+        product = base_prod if index == base_index else own_prod
         for grain in range(grains):
             at = pl.ds(side * face + grain * GRAIN, GRAIN)
-            vector = signed[s, at, offset : offset + LANES].astype(jnp.float32) * SIGN[side]
-            rest = product[s, at, :] - own_diag[s, at, :] * vector
+            rest = product[s, at, :]
             largest = jnp.max(jnp.abs(rest), axis=0, keepdims=True)
             inverse = jnp.where(largest > TINY, TOP / jnp.maximum(largest, TINY), 0.0)
             scale_out[index, slot, grain : grain + 1, :] = largest * (1.0 / TOP)
@@ -322,22 +328,146 @@
         (s, NORTH) for s in range(1, blocks)
     ]
 
+    def finish(s, side, grain, value, sweep):
+        at = pl.ds(side * face + grain * GRAIN, GRAIN)
+        if sweep < ITERS - 1:
+            signed[s, at, 0:LANES] = (value * SIGN[side]).astype(jnp.bfloat16)
+        if side in (EAST, SOUTH):
+            if sweep >= ITERS - 2:
+                total_row = sweep - (ITERS - 2)
+                sums_out[0, total_row : total_row + 1, :] += jnp.sum(
+                    value * value, axis=0, keepdims=True
+                )
+            if sweep == ITERS - 1:
+                out_at = pl.ds((side // 2) * face + grain * GRAIN, GRAIN)
+                power_ref[s, out_at, :] = value
+
+    def finish_inner(sweep):
+        for s in range(blocks - 1):
+            for grain in range(grains):
+                mask = live[s, 1, grain : grain + 1, :]
+                upper = pl.ds(SOUTH * face + grain * GRAIN, GRAIN)
+                lower = pl.ds(NORTH * face + grain * GRAIN, GRAIN)
+                both_diag = own_diag[s, upper, :] + own_diag[s + 1, lower, :]
+                vector = signed[s, upper, 0:LANES].astype(jnp.float32)
+                value = (
+                    own_prod[s, upper, :] + own_prod[s + 1, lower, :] + both_diag * vector
+                ) * mask
+                finish(s, SOUTH, grain, value, sweep)
+                if sweep < ITERS - 1:
+                    finish(s + 1, NORTH, grain, value, sweep)
+                if sweep == ITERS - 2:
+                    vector = signed[s, upper, LANES : 2 * LANES].astype(jnp.float32)
+                    base_grad[s, pl.ds(face + grain * GRAIN, GRAIN), :] = (
+                        base_prod[s, upper, :] + base_prod[s + 1, lower, :] + both_diag * vector
+                    )
+
+    def drain(sweep, block):
+        for link in links:
+            here, _, s, side, cond, _ = link
+            if s != block or (sweep == ITERS - 1 and side in (WEST, NORTH)):
+                continue
+
+            @pl.when(cond)
+            def _(link=link, here=here, s=s, side=side):
+                await_codes(link, sweep)
+                for grain in range(grains):
+                    if side in (EAST, SOUTH):
+                        mask = live[s, side // 2, grain : grain + 1, :]
+                    else:
+                        mask = info_in[here, grain : grain + 1, :]
+                    finish(s, side, grain, decode(s, side, here, sweep, grain) * mask, sweep)
+
+    def finish_base():
+        for link in owner_links:
+
+            @pl.when(link[4])
+            def _(link=link):
+                here, _, s, side = link[:4]
+                await_codes(link, base_index)
+                arrival(*modes_bufs, link).wait_recv()
+                for grain in range(grains):
+                    out_at = pl.ds((side // 2) * face + grain * GRAIN, GRAIN)
+                    base_grad[s, out_at, :] = decode(s, side, here, base_index, grain)
+
+        def coefficients(buf):
+            return jnp.concatenate(
+                [buf[0:MODE_ROWS, :], buf[MODE_ROWS : 2 * MODE_ROWS, :]], axis=1
+            )
+
+        own_coarse = [coefficients(modes_out.at[2 * blocks + 2 + s]) for s in range(blocks)]
+        for s in range(blocks):
+            for half, side in ((0, EAST), (1, SOUTH)):
+                slot = blocks + s if side == EAST else south_slot
+                if side == SOUTH and s < blocks - 1:
+                    far_coarse = own_coarse[s + 1]
+                    far_traces = traces_own[s + 1, :, (side - 1) * face : side * face]
+                else:
+                    far_coarse = coefficients(modes_in.at[slot])
+                    far_traces = jnp.concatenate(
+                        [
+                            modes_in[slot, (2 + grain) * MODE_ROWS : (3 + grain) * MODE_ROWS, :]
+                            for grain in range(grains)
+                        ],
+                        axis=1,
+                    )
+                own_traces = traces_own[s, :, side * face : (side + 1) * face]
+                part = lax.dot_general(
+                    jnp.concatenate([own_traces, -far_traces], axis=0),
+                    jnp.concatenate([own_coarse[s], far_coarse], axis=0),
+                    (((0,), (0,)), ((), ())),
+                    precision=lax.Precision.HIGHEST,
+                    preferred_element_type=jnp.float32,
+                )
+                for grain in range(grains):
+                    inner = slice(grain * GRAIN, (grain + 1) * GRAIN)
+                    out_at = pl.ds(half * face + grain * GRAIN, GRAIN)
+                    mask = live[s, half, grain : grain + 1, :]
+                    base_grad[s, out_at, :] = (
+                        base_grad[s, out_at, :] + part[inner, 0:LANES] - rhs_ref[s, out_at, :]
+                    ) * mask
+                    gap_grad[s, out_at, :] = part[inner, LANES:] * mask
+
     for sweep in range(ITERS):
         last = sweep == ITERS - 1
-        wide = sweep == 0
-        for link in links:
-            here, _, s, side, cond, _ = link
-            multiply(s, side, wide)
-            if last and side in (EAST, SOUTH):
-                continue
-
-            @pl.when(cond)
-            def _(link=link, here=here, s=s, side=side, sweep=sweep):
-                encode(s, side, here, sweep)
-                send_codes(link, sweep)
-
-        for s, side in inner_faces:
-            multiply(s, side, wide)
+        wide = sweep == ITERS - 2
+        if wide:
+            for link in far_links:
+
+                @pl.when(link[4])
+                def _(link=link):
+                    first_arrival(link, 1).wait_recv()
+
+        if sweep > 0:
+            finish_inner(sweep - 1)
+        for s in range(blocks):
+            if sweep > 0:
+                drain(sweep - 1, s)
+            ordered = [link for link in (far_links if last else links) if link[2] == s]
+            waiting = None
+            for link in ordered + [None]:
+                if link is not None:
+                    multiply(s, link[3], wide)
+                if waiting is not None:
+                    encode(s, waiting[3], waiting[0], sweep)
+
+                    @pl.when(waiting[4])
+                    def _(link=waiting, sweep=sweep):
+                        send_codes(link, sweep)
+
+                waiting = link
+            for link in owner_links if last else []:
+                if link[2] == s:
+                    multiply(s, link[3], wide)
+            for inner_s, side in inner_faces:
+                if inner_s == s:
+                    multiply(s, side, wide)
+        if sweep == 0:
+            for link in owner_links:
+
+                @pl.when(link[4])
+                def _(link=link):
+                    first_copy(link, 1).start()
 
         if wide:
             for link in far_links:
@@ -374,6 +504,7 @@
                 def _(link=link):
                     plain_copy(*modes_bufs, link).start()
 
+        if sweep == 0:
             for link in links:
 
                 @pl.when(link[4])
@@ -383,54 +514,15 @@
                     for grain in range(grains):
                         line = info_in[here, 8 + grain : 9 + grain, :]
                         line = jnp.where(eye, jnp.broadcast_to(line, (GRAIN, LANES)), 0.0)
+                        at = pl.ds(link[3] * face + grain * GRAIN, GRAIN)
                         far_diag[here, grain * GRAIN : (grain + 1) * GRAIN, :] = (
-                            jnp.broadcast_to(
-                                jnp.sum(line, axis=1, keepdims=True), (GRAIN, LANES)
-                            )
+                            own_diag[link[2], at, :] + jnp.sum(line, axis=1, keepdims=True)
                         )
 
-        def finish(s, side, grain, value, sweep=sweep, last=last):
-            at = pl.ds(side * face + grain * GRAIN, GRAIN)
-            if not last:
-                signed[s, at, 0:LANES] = (value * SIGN[side]).astype(jnp.bfloat16)
-            if side in (EAST, SOUTH):
-                if sweep >= ITERS - 2:
-                    total_row = sweep - (ITERS - 2)
-                    sums_out[0, total_row : total_row + 1, :] += jnp.sum(
-                        value * value, axis=0, keepdims=True
-                    )
-                if last:
-                    out_at = pl.ds((side // 2) * face + grain * GRAIN, GRAIN)
-                    power_ref[s, out_at, :] = value
-
-        for s in range(blocks - 1):
-            for grain in range(grains):
-                mask = live[s, 1, grain : grain + 1, :]
-                upper = pl.ds(SOUTH * face + grain * GRAIN, GRAIN)
-                lower = pl.ds(NORTH * face + grain * GRAIN, GRAIN)
-                value = (own_prod[s, upper, :] + own_prod[s + 1, lower, :]) * mask
-                finish(s, SOUTH, grain, value)
-                if not last:
-                    finish(s + 1, NORTH, grain, value)
-                if wide:
-                    base_grad[s, pl.ds(face + grain * GRAIN, GRAIN), :] = (
-                        base_prod[s, upper, :] + base_prod[s + 1, lower, :]
-                    )
-
-        for link in links:
-            here, _, s, side, cond, _ = link
-            if last and side in (WEST, NORTH):
-                continue
-
-            @pl.when(cond)
-            def _(link=link, here=here, s=s, side=side, sweep=sweep, finish=finish):
-                await_codes(link, sweep)
-                for grain in range(grains):
-                    if side in (EAST, SOUTH):
-                        mask = live[s, side // 2, grain : grain + 1, :]
-                    else:
-                        mask = info_in[here, grain : grain + 1, :]
-                    finish(s, side, grain, decode(s, side, here, sweep, grain) * mask)
+    finish_base()
+    finish_inner(ITERS - 1)
+    for s in range(blocks):
+        drain(ITERS - 1, s)
 
     sums_col[col] = sums_out[0]
     col_copies = []
@@ -444,17 +536,6 @@
         )
         copy.start()
         col_copies.append(copy)
-
-    for link in owner_links:
-
-        @pl.when(link[4])
-        def _(link=link):
-            here, _, s, side = link[:4]
-            await_codes(link, base_index)
-            arrival(*modes_bufs, link).wait_recv()
-            for grain in range(grains):
-                out_at = pl.ds((side // 2) * face + grain * GRAIN, GRAIN)
-                base_grad[s, out_at, :] = decode(s, side, here, base_index, grain)
 
     for copy in col_copies:
         copy.wait()
@@ -482,40 +563,18 @@
     step_length = 1.9 / penalty
     inverse_norm = 1.0 / jnp.sqrt(newest + EPSILON)
 
-    def coefficients(buf):
-        return buf[0:MODE_ROWS, :] + penalty * buf[MODE_ROWS : 2 * MODE_ROWS, :]
-
-    own_coarse = [coefficients(modes_out.at[2 * blocks + 2 + s]) for s in range(blocks)]
     for s in range(blocks):
-        new_coarse_ref[s] = own_coarse[s][0:modes, :]
+        buf = modes_out.at[2 * blocks + 2 + s]
+        new_coarse_ref[s] = (
+            buf[0:modes, :] + penalty * buf[MODE_ROWS : MODE_ROWS + modes, :]
+        )
     for s in range(blocks):
-        for half, side in ((0, EAST), (1, SOUTH)):
-            slot = blocks + s if side == EAST else south_slot
-            local = side == SOUTH and s < blocks - 1
-            far_coarse = own_coarse[s + 1] if local else coefficients(modes_in.at[slot])
-            pair = jnp.concatenate([own_coarse[s], far_coarse], axis=0)
+        for half in range(2):
             hit = (contact_ref[s, half] > 0).astype(jnp.float32)
             for grain in range(grains):
-                at = side * face + grain * GRAIN
-                if local:
-                    far_at = at - face
-                    far_traces = traces_own[s + 1, :, far_at : far_at + GRAIN]
-                else:
-                    base_row = (2 + grain) * MODE_ROWS
-                    far_traces = modes_in[slot, base_row : base_row + MODE_ROWS, :]
-                both = jnp.concatenate(
-                    [traces_own[s, :, at : at + GRAIN], -far_traces], axis=0
-                )
-                coarse_part = lax.dot_general(
-                    both,
-                    pair,
-                    (((0,), (0,)), ((), ())),
-                    precision=lax.Precision.HIGHEST,
-                    preferred_element_type=jnp.float32,
-                )
                 out_at = pl.ds(half * face + grain * GRAIN, GRAIN)
                 mask = live[s, half, grain : grain + 1, :]
-                grad = (base_grad[s, out_at, :] + coarse_part - rhs_ref[s, out_at, :]) * mask
+                grad = base_grad[s, out_at, :] + penalty * gap_grad[s, out_at, :]
                 trial = mult_ref[s, out_at, :] * mask - step_length * grad
                 clipped = jnp.maximum(trial, 0.0)
                 new_mult_ref[s, out_at, :] = jnp.where(hit > 0.0, clipped, trial) * mask
@@ -532,7 +591,8 @@
                 plain_copy(*scale_bufs, link, index).wait_send()
                 plain_copy(*code_bufs, link, index).wait_send()
             if owner:
-                first_copy(link).wait_send()
+                first_copy(link, 0).wait_send()
+                first_copy(link, 1).wait_send()
             else:
                 plain_copy(*modes_bufs, link).wait_send()
 
@@ -577,9 +637,10 @@
         scratch_shapes=[
             pltpu.VMEM((blocks, order_size, order_size), bf16),
             pltpu.VMEM((blocks, order_size, 2 * columns), bf16),
-            pltpu.VMEM((slots, face, 2 * columns), bf16),
+            pltpu.VMEM((2, slots, face, columns), bf16),
             pltpu.VMEM((blocks, order_size, columns), f32),
             pltpu.VMEM((blocks, order_size, columns), f32),
+            pltpu.VMEM((blocks, owned_len, columns), f32),
             pltpu.VMEM((blocks, owned_len, columns), f32),
             pltpu.VMEM((blocks, order_size, columns), f32),
             pltpu.VMEM((slots, face, columns), f32),
@@ -597,8 +658,8 @@
             pltpu.VMEM((mesh_cols, 8, columns), f32),
             pltpu.VMEM((mesh_rows, 8, columns), f32),
             dma((blocks,)),
-            dma((slots,)),
-            dma((slots,)),
+            dma((2, slots)),
+            dma((2, slots)),
             dma((slots,)),
             dma((slots,)),
             dma((ITERS + 1, slots)),

time: 114 us -> 106 us (0.930)
  Pallas kernels: 101 us -> 92.4 us
    pallas_call x1, Pallas kernels: 101 us -> 92.4 us  [body(): pl.pallas_call(functools.partial(kernel, mesh_rows, mesh_cols), out_shape...]
where the time goes in v2:
time: 106 us; the launch traced here: 105 us
  Pallas kernels  92.4 us (87%)
  local copies, waits for them, and re-layouts  12.2 us (12%)
    pallas_call x1, Pallas kernels, body(): pl.pallas_call(functools.partial(kernel, mesh_rows, mesh_cols), out_shape...  92.4 us
    unnamed x8, local copies, waits for them, and re-layouts  11 us

profile of v2, /device:TPU:0, one launch (start us, length us, event | category | flops | bytes accessed | tf_op | source)
XLA Modules:
  0.0 105.2 jit_solution(6193085658364234693)
XLA Ops:
  0.6 1.3 %copy.24.count_ref = s32[2,1]{1,0:T(2,128)} copy(s32[2,1]{0,1:T(1,128)} %param.19) | data formatting | bytes 16 | tf_op args[9]
  1.9 0.7 copy.33
  2.6 0.6 copy.22.coarse_mult_ref
  3.2 0.7 copy.32
  3.9 0.6 copy.23.coarse_rhs_ref
  4.5 1.4 %copy.31 = bf16[2,1,6,2048]{3,2,0,1:T(8,128)(2,1)} copy(bf16[2,1,6,2048]{3,0,2,1:T(2,128)(2,1)} %param.14) | data formatting | bytes 98304 | tf_op args[4]
  6.0 92.4 %shard_map.129 = (f32[2,1024,128]{2,1,0:T(8,128)}, f32[2,1024,128]{2,1,0:T(8,128)}, f32[1,128]{1,0:T(1,128)}, f32[2,6,128]{2,1,0:T(8,128)}) custom-call(bf16[2,2048,2048]{2,1,0:T(8,128)(2,1)} %bitcast.29, f32[2,1024,128]{2,1,0:T(8,128)} %bitcast.30, f32[2,1024,128]{2,1,0:T(8,128)} %bitcast.31, f32[2,1024,128]{2,1,0:T(8,128)} %bitcast.32, ...), custom_call_target="tpu_custom_call" | custom-call | flops 10737418240 | bytes 16777216 | tf_op jit(solution)/shard_map/pallas_call | solution.py:627
  98.3 1.3 %copy.27 = f32[2,1,6,128]{3,1,2,0:T(1,128)} copy(f32[2,1,6,128]{3,2,0,1:T(8,128)} %bitcast.28) | data formatting | bytes 12288
  99.6 2.3 %copy.37 = f32[2,1,1024,128]{3,2,1,0:T(8,128)} copy(f32[2,1,1024,128]{3,2,1,0:T(8,128)} %bitcast.24) | data formatting | bytes 2097152
  101.9 2.3 %copy.38 = f32[2,1,1024,128]{3,2,1,0:T(8,128)} copy(f32[2,1,1024,128]{3,2,1,0:T(8,128)} %bitcast.23) | data formatting | bytes 2097152
  104.2 1.1 %copy.39 = f32[128]{0:T(128)} copy(f32[128]{0:T(128)} %bitcast.35) | data formatting | bytes 1024
